TPU v7x, 256 devices: a whole 4x4x8 slice. The times are simulated.
256 devices in a mesh: rep: 32 (over y, x, core), fsdp: 8 (over z).
Axes of the slice: x: 4, y: 4, z: 8, core: 2. Of those that a mesh axis runs over, the one named last changes fastest.
Arguments:
- codes: bfloat16 [32, 4096, 1024], P('rep', 'fsdp'), may hold values from -127 to 127
- block_scales: float32 [32, 4096, 8], P('rep', 'fsdp'), may hold values from 0.002 to 0.02
- params: bfloat16 [4096, 1024], P('fsdp'), may hold values from -6 to 6
- momentum: bfloat16 [4096, 1024], P('fsdp'), may hold values from -3 to 3
Outputs:
- new_params: bfloat16 [4096, 1024], replicated
- new_momentum: bfloat16 [4096, 1024], P('fsdp')
All inputs are finite; a program needn't handle non-finite values.
Results may differ from a plain program's by a relative error of at most 0.006.
Values may be sent and summed in bfloat16 or wider, within the bound.
A program may use at most 64 MiB of HBM per device.

v0:
```python
import jax
import jax.numpy as jnp
from jax import lax
from jax.sharding import Mesh
from jax.sharding import PartitionSpec as P

REP = ("rep_0", "rep_1", "rep_2")


def filled_up(lines, peers):
    spare = -len(lines) % peers
    return jnp.pad(lines, [(0, spare)] + [(0, 0)] * (lines.ndim - 1))


def sent_to_all(shard, axis):
    copies = jnp.broadcast_to(shard, (lax.axis_size(axis), *shard.shape))
    return lax.all_to_all(copies, axis, split_axis=0, concat_axis=0, tiled=True)


def joined_along(blocks, dim):
    blocks = jnp.moveaxis(blocks, 0, dim)
    lengths = blocks.shape
    return blocks.reshape(*lengths[:dim], lengths[dim] * lengths[dim + 1], *lengths[dim + 2 :])


def whole_of(shard, axes, dim):
    far, near = axes
    first = sent_to_all(shard, far)
    blocks = jnp.swapaxes(sent_to_all(first, near), 0, 1)
    return joined_along(blocks.reshape(-1, *shard.shape), dim)


def in_blocks(shard, dim, peers):
    before, after = (shard.shape[:dim], shard.shape[dim + 1 :])
    return jnp.moveaxis(shard.reshape(*before, peers, -1, *after), dim, 0)


def sum_at_owner(shard, axis, dim):
    blocks = in_blocks(shard, dim, lax.axis_size(axis))
    arrived = lax.all_to_all(blocks, axis, split_axis=0, concat_axis=0, tiled=True)
    return arrived.astype(jnp.float32).sum(axis=0)


def summed_rows(shard, axes, dim):
    far, near = axes
    own = sum_at_owner(in_blocks(shard, dim, lax.axis_size(far)), near, dim + 1)
    return jnp.sum(
        lax.all_to_all(own.astype(jnp.bfloat16), far, 0, 0, tiled=True).astype(jnp.float32), axis=0
    )


def sum_by_parts(shard, axes):
    lines = shard.reshape(-1, shard.shape[-1])
    padded = filled_up(lines, lax.axis_size(axes[0]) * lax.axis_size(axes[1]))
    whole = whole_of(summed_rows(padded, axes, 0).astype(jnp.bfloat16), axes, 0)
    return lax.slice_in_dim(whole, 0, len(lines)).reshape(shard.shape).astype(jnp.float32)


def dequantize(code_rows, scale_rows):
    count, width = code_rows.shape
    pieces = (
        code_rows.astype(jnp.float32).reshape(count, width // 128, 128) * scale_rows[:, :, None]
    )
    return pieces.reshape(count, width)


def outer_update(total, params, momentum, replicas):
    delta = total / replicas
    moment = 0.9 * momentum.astype(jnp.float32) + delta
    updated = (params.astype(jnp.float32) - 0.7 * (delta + 0.9 * moment)).astype(jnp.bfloat16)
    return (updated, moment.astype(jnp.bfloat16))


def local(codes, block_scales, params, momentum):
    replicas = lax.axis_size(REP)
    local_term = dequantize(codes[0], block_scales[0])
    total = sum_by_parts(local_term.astype(jnp.bfloat16), (("rep_0", "rep_1"), "rep_2"))
    updated, new_momentum = outer_update(total, params, momentum, replicas)
    new_params = lax.all_gather(updated, "fsdp", axis=0, tiled=True)
    return (new_params, new_momentum)


def solution(mesh):
    finer = Mesh(
        mesh.devices.reshape(4, 4, 2, mesh.shape["fsdp"]), ("rep_0", "rep_1", "rep_2", "fsdp")
    )
    placed = (P(REP, "fsdp", None), P(REP, "fsdp", None), P("fsdp", None), P("fsdp", None))
    return jax.shard_map(
        local, mesh=finer, in_specs=placed, out_specs=(P(), P("fsdp", None)), check_vma=False
    )
```

profile of v0, /device:TPU:1, one launch (start us, length us, event | category | flops | bytes accessed | tf_op | source)
XLA Modules:
  0.0 167.0 jit_solution(15279222004547587232)
XLA Ops:
  7.2 0.0 all-gather.2.cloned.1.call-start
  7.2 0.8 copy.11
  8.1 0.6 mul.27
  8.7 0.0 copy-start
  8.7 1.5 mul.28
  10.2 0.0 copy-done
  10.2 1.9 %fusion.5 = bf16[2,16,16,1024]{3,2,0,1:T(8,128)(2,1)S(1)} fusion(f32[16,2,16,1024]{3,2,1,0:T(8,128)} %mul.28, bf16[16,2,16,1024]{3,2,1,0:T(8,128)(2,1)S(1)} %bitcast.20), kind=kLoop, calls=%fused_computation.9 | loop fusion | flops 1572864 | bytes 4194304 | tf_op jit(solution)/shard_map/transpose | solution.py:35
  12.1 0.1 copy.12
  12.2 7.4 %all_to_all.20 = bf16[2,16,16,1024]{3,2,1,0:T(8,128)(2,1)S(1)} all-to-all(bf16[2,16,16,1024]{3,2,1,0:T(8,128)(2,1)S(1)} %copy.12), channel_id=1, replica_groups=mesh['rep_0'=4,'rep_1'=4,'rep_2'=2,'fsdp'=8] {'rep_2'}, dimensions={0} | all-to-all | bytes 2097152 | tf_op jit(solution)/shard_map/all_to_all | solution.py:40
  19.6 0.3 reduce_sum.24
  19.9 15.5 %all_to_all.21 = bf16[16,16,1024]{2,1,0:T(8,128)(2,1)S(1)} all-to-all(bf16[16,16,1024]{2,1,0:T(8,128)(2,1)S(1)} %reduce_sum.24), channel_id=1, replica_groups=mesh['rep_0'=4,'rep_1'=4,'rep_2'=2,'fsdp'=8] {'rep_0','rep_1'}, dimensions={0} | all-to-all | bytes 1048576 | tf_op jit(solution)/shard_map/all_to_all | solution.py:48
  35.4 0.1 reduce_sum.25
  35.5 0.1 broadcast_in_dim.6
  35.6 13.4 %all_to_all.22 = bf16[16,16,1024]{2,1,0:T(8,128)(2,1)S(1)} all-to-all(bf16[16,16,1024]{2,1,0:T(8,128)(2,1)S(1)} %broadcast_in_dim.6), channel_id=1, replica_groups=mesh['rep_0'=4,'rep_1'=4,'rep_2'=2,'fsdp'=8] {'rep_0','rep_1'}, dimensions={0} | all-to-all | bytes 1048576 | tf_op jit(solution)/shard_map/all_to_all | solution.py:17
  49.0 0.1 broadcast_in_dim.7
  49.1 6.5 %all_to_all.23 = bf16[2,16,16,1024]{3,2,1,0:T(8,128)(2,1)S(1)} all-to-all(bf16[2,16,16,1024]{3,2,1,0:T(8,128)(2,1)S(1)} %broadcast_in_dim.7), channel_id=1, replica_groups=mesh['rep_0'=4,'rep_1'=4,'rep_2'=2,'fsdp'=8] {'rep_2'}, dimensions={0} | all-to-all | bytes 2097152 | tf_op jit(solution)/shard_map/all_to_all | solution.py:17
  55.7 0.0 copy-start.1
  55.7 0.3 convert_multiply_fusion.1
  55.9 1.0 copy-done.1
  56.9 0.3 copy-done.2
  57.2 2.0 %fusion.4 = (bf16[512,1024]{1,0:T(8,128)(2,1)}, bf16[512,1024]{1,0:T(8,128)(2,1)}) fusion(f32[2,16,16,1024]{3,2,0,1:T(8,128)S(1)} %convert_multiply_fusion.1, bf16[512,1024]{1,0:T(8,128)(2,1)S(1)} %copy-done.1, bf16[512,1024]{1,0:T(8,128)(2,1)S(1)} %copy-done.2), kind=kLoop, calls=%fused_computation.7 | loop fusion | flops 5242880 | bytes 6291456 | tf_op jit(solution)/shard_map/convert_element_type | solution.py:71
  59.3 0.0 all-gather.2.cloned.1.call-update
  59.3 93.1 %all-gather.2.cloned.1.call-done = bf16[4096,1024]{1,0:T(8,128)(2,1)} async-done(((bf16[512,1024]{1,0:T(8,128)(2,1)}), bf16[4096,1024]{1,0:T(8,128)(2,1)}) %all-gather.2.cloned.1.call-update) | async-done | bytes 8388624 | tf_op jit(solution)/shard_map/all_gather | solution.py:79
  152.4 7.8 %copy.16 = bf16[4096,1024]{1,0:T(8,128)(2,1)} copy(bf16[4096,1024]{1,0:T(8,128)(2,1)} %all-gather.2.cloned.1.call-done) | data formatting | bytes 16777216
  (1 shorter events, 0.0 us)
Async XLA Ops:
  7.2 145.2 %all-gather.2.cloned.1.call-start = ((), (), s32[]{:S(2)}) async-start(), calls=%async_computation.4 | async-start | bytes 9437184 | tf_op jit(solution)/shard_map/all_gather | solution.py:79
  8.7 1.5 copy-start
  55.7 1.2 copy-start.1
  55.7 1.5 copy-start.2
Sparse Core Ops, SparseCore 0:
  59.4 92.9 all-gather.1
where the time goes:
time: 167 us
  waiting for transfers between devices  93.1 us (56%)
  blocking collectives  42.9 us (26%)
  between operations  14.1 us (8%)
  local copies, waits for them, and re-layouts  12.2 us (7%)
  other arithmetic  4.57 us (3%)
    all_gather x1, waiting for transfers between devices, local(): new_params = lax.all_gather(updated, 'fsdp', axis=0, tiled=True)  93.1 us
    all_to_all x2, blocking collectives, sent_to_all(): return lax.all_to_all(copies, axis, split_axis=0, concat_axis=0, tiled=True)  20 us
    all_to_all x1, blocking collectives, summed_rows(): lax.all_to_all(own.astype(jnp.bfloat16), far, 0, 0, tiled=True)  15.5 us
    unnamed x7, local copies, waits for them, and re-layouts  9.05 us
    all_to_all x1, blocking collectives, sum_at_owner(): lax.all_to_all(blocks, axis, split_axis=0, concat_axis=0, tiled=True)  7.44 us
  transfers between devices with their start and end apart: 1, of which 1 were waited for; matrix products, arithmetic and copies ran while one was open for 0% of the time, Pallas kernels for 0%

commit v1 on v0

--- a/solution.py
+++ b/solution.py
@@ -5,6 +5,27 @@
 from jax.sharding import PartitionSpec as P
 
 REP = ("rep_0", "rep_1", "rep_2")
+
+
+def ring_gather(array, axis, dim):
+    size, index, rows = (lax.axis_size(axis), lax.axis_index(axis), array.shape[dim])
+    ahead = [(i, (i + 1) % size) for i in range(size)]
+    behind = [(i, (i - 1) % size) for i in range(size)]
+    filled = jnp.zeros((*array.shape[:dim], size * rows, *array.shape[dim + 1 :]), array.dtype)
+    filled = lax.dynamic_update_slice_in_dim(filled, array, index * rows, axis=dim)
+    from_left = from_right = array
+    middle = size // 2
+    for lap in range(1, middle + 1):
+        from_left = lax.ppermute(from_left, axis, ahead)
+        filled = lax.dynamic_update_slice_in_dim(
+            filled, from_left, (index - lap) % size * rows, axis=dim
+        )
+        if lap < size - middle:
+            from_right = lax.ppermute(from_right, axis, behind)
+            filled = lax.dynamic_update_slice_in_dim(
+                filled, from_right, (index + lap) % size * rows, axis=dim
+            )
+    return filled
 
 
 def filled_up(lines, peers):
@@ -76,7 +97,7 @@
     local_term = dequantize(codes[0], block_scales[0])
     total = sum_by_parts(local_term.astype(jnp.bfloat16), (("rep_0", "rep_1"), "rep_2"))
     updated, new_momentum = outer_update(total, params, momentum, replicas)
-    new_params = lax.all_gather(updated, "fsdp", axis=0, tiled=True)
+    new_params = ring_gather(updated, "fsdp", 0)
     return (new_params, new_momentum)
 
 

time: 167 us -> 159 us (0.952)
  between operations: 14.1 us -> 0.83 us
  starting transfers between devices: 0.04 us -> 9.98 us
  waiting for transfers between devices: 93.1 us -> 84.9 us
  local copies, waits for them, and re-layouts: 12.2 us -> 14.4 us
    all_gather x1 -> x0, waiting for transfers between devices: 93.1 us -> none  [local(): new_params = lax.all_gather(updated, 'fsdp', axis=0, tiled=True)]
    ppermute x0 -> x7, waiting for transfers between devices: none -> 84.9 us  [the longest x4 84.9 us: ring_gather(): from_left = lax.ppermute(from_left, axis, ahead)]
    ppermute x0 -> x7, starting transfers between devices: none -> 9.98 us  [the longest x3 8.33 us: ring_gather(): from_right = lax.ppermute(from_right, axis, behind)]
    dynamic_update_slice x0 -> x8, local copies, waits for them, and re-layouts: none -> 5.78 us  [the longest x4 2.89 us: ring_gather(): lax.dynamic_update_slice_in_dim(filled, from_left, (index - lap) % size *...]
    unnamed x7 -> x10, local copies, waits for them, and re-layouts: 9.05 us -> 4.37 us
  transfers between devices with their start and end apart: 1 -> 7, of which waited for: 1 -> 4; matrix products, arithmetic and copies ran while one was open for 0% -> 3% of each run, Pallas kernels for 0% -> 0%
where the time goes in v1:
time: 159 us; the launch traced here: 158 us
  waiting for transfers between devices  84.9 us (53%)
  blocking collectives  43.2 us (27%)
  local copies, waits for them, and re-layouts  14.4 us (9%)
  starting transfers between devices  9.98 us (6%)
  other arithmetic  4.5 us (3%)
    ppermute x4, waiting for transfers between devices, ring_gather(): from_left = lax.ppermute(from_left, axis, ahead)  84.9 us
    all_to_all x2, blocking collectives, sent_to_all(): return lax.all_to_all(copies, axis, split_axis=0, concat_axis=0, tiled=True)  20.1 us
    all_to_all x1, blocking collectives, summed_rows(): lax.all_to_all(own.astype(jnp.bfloat16), far, 0, 0, tiled=True)  15.5 us
    ppermute x3, starting transfers between devices, ring_gather(): from_right = lax.ppermute(from_right, axis, behind)  8.33 us
    all_to_all x1, blocking collectives, sum_at_owner(): lax.all_to_all(blocks, axis, split_axis=0, concat_axis=0, tiled=True)  7.57 us
    unnamed x10, local copies, waits for them, and re-layouts  4.37 us
  transfers between devices with their start and end apart: 7, of which 4 were waited for; matrix products, arithmetic and copies ran while one was open for 3% of the time, Pallas kernels for 0%

profile of v1, /device:TPU:1, one launch (start us, length us, event | category | flops | bytes accessed | tf_op | source)
XLA Modules:
  0.0 157.8 jit_solution(3993037455809358906)
XLA Ops:
  0.6 0.8 copy.11
  1.5 0.6 mul.51
  2.1 1.5 mul.52
  3.6 2.2 %fusion.5 = bf16[2,16,16,1024]{3,2,0,1:T(8,128)(2,1)S(1)} fusion(f32[16,2,16,1024]{3,2,1,0:T(8,128)} %mul.52, bf16[16,2,16,1024]{3,2,1,0:T(8,128)(2,1)} %bitcast.20), kind=kLoop, calls=%fused_computation.9 | loop fusion | flops 1572864 | bytes 4194304 | tf_op jit(solution)/shard_map/transpose | solution.py:56
  5.9 7.6 %all_to_all.20 = bf16[2,16,16,1024]{3,2,1,0:T(8,128)(2,1)S(1)} all-to-all(bf16[2,16,16,1024]{3,2,1,0:T(8,128)(2,1)S(1)} %copy.12), channel_id=1, replica_groups=mesh['rep_0'=4,'rep_1'=4,'rep_2'=2,'fsdp'=8] {'rep_2'}, dimensions={0} | all-to-all | bytes 2097152 | tf_op jit(solution)/shard_map/all_to_all | solution.py:61
  13.7 15.5 %all_to_all.21 = bf16[16,16,1024]{2,1,0:T(8,128)(2,1)S(1)} all-to-all(bf16[16,16,1024]{2,1,0:T(8,128)(2,1)S(1)} %reduce_sum.24), channel_id=1, replica_groups=mesh['rep_0'=4,'rep_1'=4,'rep_2'=2,'fsdp'=8] {'rep_0','rep_1'}, dimensions={0} | all-to-all | bytes 1048576 | tf_op jit(solution)/shard_map/all_to_all | solution.py:69
  29.4 13.6 %all_to_all.22 = bf16[16,16,1024]{2,1,0:T(8,128)(2,1)S(1)} all-to-all(bf16[16,16,1024]{2,1,0:T(8,128)(2,1)S(1)} %broadcast_in_dim.10), channel_id=1, replica_groups=mesh['rep_0'=4,'rep_1'=4,'rep_2'=2,'fsdp'=8] {'rep_0','rep_1'}, dimensions={0} | all-to-all | bytes 1048576 | tf_op jit(solution)/shard_map/all_to_all | solution.py:38
  43.1 6.5 %all_to_all.23 = bf16[2,16,16,1024]{3,2,1,0:T(8,128)(2,1)S(1)} all-to-all(bf16[2,16,16,1024]{3,2,1,0:T(8,128)(2,1)S(1)} %broadcast_in_dim.11), channel_id=1, replica_groups=mesh['rep_0'=4,'rep_1'=4,'rep_2'=2,'fsdp'=8] {'rep_2'}, dimensions={0} | all-to-all | bytes 2097152 | tf_op jit(solution)/shard_map/all_to_all | solution.py:38
  49.9 1.7 %fusion.4 = (bf16[512,1024]{1,0:T(8,128)(2,1)}, bf16[512,1024]{1,0:T(8,128)(2,1)S(1)}) fusion(f32[2,16,16,1024]{3,2,0,1:T(8,128)S(1)} %convert_multiply_fusion.1, bf16[512,1024]{1,0:T(8,128)(2,1)S(1)} %copy-done.3, bf16[512,1024]{1,0:T(8,128)(2,1)S(1)} %copy-done.4), kind=kLoop, calls=%fused_computation.7 | loop fusion | flops 5242880 | bytes 6291456 | tf_op jit(solution)/shard_map/convert_element_type | solution.py:92
  51.6 1.6 %collective-permute-start = (bf16[512,1024]{1,0:T(8,128)(2,1)S(1)}, bf16[512,1024]{1,0:T(8,128)(2,1)S(1)}, u32[]{:S(2)}, u32[]{:S(2)}) collective-permute-start(bf16[512,1024]{1,0:T(8,128)(2,1)S(1)} %get-tuple-element.3), channel_id=1, source_target_pairs={{0,1},{1,2},{2,3},{3,4},{4,5},{5,6},{6,7},{7,0},{8,9},{9,10},{10,1... | collective-permute-start | bytes 3145736 | tf_op jit(solution)/shard_map/ppermute | solution.py:19
  53.2 3.9 %collective-permute-start.1 = (bf16[512,1024]{1,0:T(8,128)(2,1)S(1)}, bf16[512,1024]{1,0:T(8,128)(2,1)S(1)}, u32[]{:S(2)}, u32[]{:S(2)}) collective-permute-start(bf16[512,1024]{1,0:T(8,128)(2,1)S(1)} %get-tuple-element.3), channel_id=1, source_target_pairs={{0,7},{1,0},{2,1},{3,2},{4,3},{5,4},{6,5},{7,6},{8,15},{9,8},{10,9... | collective-permute-start | bytes 3145736 | tf_op jit(solution)/shard_map/ppermute | solution.py:24
  57.2 23.2 %collective-permute-done = bf16[512,1024]{1,0:T(8,128)(2,1)S(1)} collective-permute-done((bf16[512,1024]{1,0:T(8,128)(2,1)S(1)}, bf16[512,1024]{1,0:T(8,128)(2,1)S(1)}, u32[]{:S(2)}, u32[]{:S(2)}) %collective-permute-start) | collective-permute-done | bytes 1048608 | tf_op jit(solution)/shard_map/ppermute | solution.py:19
  80.4 2.7 %collective-permute-start.3 = (bf16[512,1024]{1,0:T(8,128)(2,1)S(1)}, bf16[512,1024]{1,0:T(8,128)(2,1)}, u32[]{:S(2)}, u32[]{:S(2)}) collective-permute-start(bf16[512,1024]{1,0:T(8,128)(2,1)S(1)} %collective-permute-done.1), channel_id=1, source_target_pairs={{0,7},{1,0},{2,1},{3,2},{4,3},{5,4},{6,5},{7,6},{8,15},{9,8},{10,9... | collective-permute-start | bytes 3145736 | tf_op jit(solution)/shard_map/ppermute | solution.py:24
  83.1 22.3 %collective-permute-done.2 = bf16[512,1024]{1,0:T(8,128)(2,1)S(1)} collective-permute-done((bf16[512,1024]{1,0:T(8,128)(2,1)S(1)}, bf16[512,1024]{1,0:T(8,128)(2,1)S(1)}, u32[]{:S(2)}, u32[]{:S(2)}) %collective-permute-start.2) | collective-permute-done | bytes 1048608 | tf_op jit(solution)/shard_map/ppermute | solution.py:19
  105.4 1.0 copy-done.1
  106.4 1.7 %collective-permute-start.5 = (bf16[512,1024]{1,0:T(8,128)(2,1)}, bf16[512,1024]{1,0:T(8,128)(2,1)}, u32[]{:S(2)}, u32[]{:S(2)}) collective-permute-start(bf16[512,1024]{1,0:T(8,128)(2,1)} %collective-permute-done.3), channel_id=1, source_target_pairs={{0,7},{1,0},{2,1},{3,2},{4,3},{5,4},{6,5},{7,6},{8,15},{9,8},{10,9... | collective-permute-start | bytes 3145736 | tf_op jit(solution)/shard_map/ppermute | solution.py:24
  108.1 21.5 %collective-permute-done.4 = bf16[512,1024]{1,0:T(8,128)(2,1)} collective-permute-done((bf16[512,1024]{1,0:T(8,128)(2,1)S(1)}, bf16[512,1024]{1,0:T(8,128)(2,1)}, u32[]{:S(2)}, u32[]{:S(2)}) %collective-permute-start.4) | collective-permute-done | bytes 1048608 | tf_op jit(solution)/shard_map/ppermute | solution.py:19
  129.6 1.1 broadcast_in_dim.9
  131.2 1.3 constant_dynamic-update-slice_fusion.3
  132.5 1.3 constant_dynamic-update-slice_fusion.2
  133.9 1.3 constant_dynamic-update-slice_fusion.1
  135.2 17.9 %collective-permute-done.6 = bf16[512,1024]{1,0:T(8,128)(2,1)} collective-permute-done((bf16[512,1024]{1,0:T(8,128)(2,1)}, bf16[512,1024]{1,0:T(8,128)(2,1)}, u32[]{:S(2)}, u32[]{:S(2)}) %collective-permute-start.6) | collective-permute-done | bytes 1048608 | tf_op jit(solution)/shard_map/ppermute | solution.py:19
  153.1 1.3 constant_dynamic-update-slice_fusion
  154.4 3.4 %copy-done = bf16[4096,1024]{1,0:T(8,128)(2,1)} copy-done((bf16[4096,1024]{1,0:T(8,128)(2,1)}, bf16[4096,1024]{1,0:T(8,128)(2,1)S(1)}, u32[]{:S(2)}) %copy-start) | copy-done | bytes 8388632
  (24 shorter events, 1.3 us)
Async XLA Ops:
  5.8 44.1 %copy-start.3 = (bf16[512,1024]{1,0:T(8,128)(2,1)S(1)}, bf16[512,1024]{1,0:T(8,128)(2,1)}, u32[]{:S(2)}) copy-start(bf16[512,1024]{1,0:T(8,128)(2,1)} %param.7) | copy-start | bytes 3145732
  29.3 20.6 %copy-start.4 = (bf16[512,1024]{1,0:T(8,128)(2,1)S(1)}, bf16[512,1024]{1,0:T(8,128)(2,1)}, u32[]{:S(2)}) copy-start(bf16[512,1024]{1,0:T(8,128)(2,1)} %param.6) | copy-start | bytes 3145732
  51.6 28.8 %collective-permute-start = (bf16[512,1024]{1,0:T(8,128)(2,1)S(1)}, bf16[512,1024]{1,0:T(8,128)(2,1)S(1)}, u32[]{:S(2)}, u32[]{:S(2)}) collective-permute-start(bf16[512,1024]{1,0:T(8,128)(2,1)S(1)} %get-tuple-element.3), channel_id=1, source_target_pairs={{0,1},{1,2},{2,3},{3,4},{4,5},{5,6},{6,7},{7,0},{8,9},{9,10},{10,1... | collective-permute-start | bytes 3145736 | tf_op jit(solution)/shard_map/ppermute | solution.py:19
  53.2 27.2 %collective-permute-start.1 = (bf16[512,1024]{1,0:T(8,128)(2,1)S(1)}, bf16[512,1024]{1,0:T(8,128)(2,1)S(1)}, u32[]{:S(2)}, u32[]{:S(2)}) collective-permute-start(bf16[512,1024]{1,0:T(8,128)(2,1)S(1)} %get-tuple-element.3), channel_id=1, source_target_pairs={{0,7},{1,0},{2,1},{3,2},{4,3},{5,4},{6,5},{7,6},{8,15},{9,8},{10,9... | collective-permute-start | bytes 3145736 | tf_op jit(solution)/shard_map/ppermute | solution.py:24
  80.4 25.0 %collective-permute-start.2 = (bf16[512,1024]{1,0:T(8,128)(2,1)S(1)}, bf16[512,1024]{1,0:T(8,128)(2,1)S(1)}, u32[]{:S(2)}, u32[]{:S(2)}) collective-permute-start(bf16[512,1024]{1,0:T(8,128)(2,1)S(1)} %collective-permute-done), channel_id=1, source_target_pairs={{0,1},{1,2},{2,3},{3,4},{4,5},{5,6},{6,7},{7,0},{8,9},{9,10},{10,1... | collective-permute-start | bytes 3145736 | tf_op jit(solution)/shard_map/ppermute | solution.py:19
  80.4 25.0 %collective-permute-start.3 = (bf16[512,1024]{1,0:T(8,128)(2,1)S(1)}, bf16[512,1024]{1,0:T(8,128)(2,1)}, u32[]{:S(2)}, u32[]{:S(2)}) collective-permute-start(bf16[512,1024]{1,0:T(8,128)(2,1)S(1)} %collective-permute-done.1), channel_id=1, source_target_pairs={{0,7},{1,0},{2,1},{3,2},{4,3},{5,4},{6,5},{7,6},{8,15},{9,8},{10,9... | collective-permute-start | bytes 3145736 | tf_op jit(solution)/shard_map/ppermute | solution.py:24
  105.4 1.0 copy-start.1
  105.4 24.2 %collective-permute-start.4 = (bf16[512,1024]{1,0:T(8,128)(2,1)S(1)}, bf16[512,1024]{1,0:T(8,128)(2,1)}, u32[]{:S(2)}, u32[]{:S(2)}) collective-permute-start(bf16[512,1024]{1,0:T(8,128)(2,1)S(1)} %collective-permute-done.2), channel_id=1, source_target_pairs={{0,1},{1,2},{2,3},{3,4},{4,5},{5,6},{6,7},{7,0},{8,9},{9,10},{10,1... | collective-permute-start | bytes 3145736 | tf_op jit(solution)/shard_map/ppermute | solution.py:19
  106.4 27.5 %collective-permute-start.5 = (bf16[512,1024]{1,0:T(8,128)(2,1)}, bf16[512,1024]{1,0:T(8,128)(2,1)}, u32[]{:S(2)}, u32[]{:S(2)}) collective-permute-start(bf16[512,1024]{1,0:T(8,128)(2,1)} %collective-permute-done.3), channel_id=1, source_target_pairs={{0,7},{1,0},{2,1},{3,2},{4,3},{5,4},{6,5},{7,6},{8,15},{9,8},{10,9... | collective-permute-start | bytes 3145736 | tf_op jit(solution)/shard_map/ppermute | solution.py:24
  129.6 23.5 %collective-permute-start.6 = (bf16[512,1024]{1,0:T(8,128)(2,1)}, bf16[512,1024]{1,0:T(8,128)(2,1)}, u32[]{:S(2)}, u32[]{:S(2)}) collective-permute-start(bf16[512,1024]{1,0:T(8,128)(2,1)} %collective-permute-done.4), channel_id=1, source_target_pairs={{0,1},{1,2},{2,3},{3,4},{4,5},{5,6},{6,7},{7,0},{8,9},{9,10},{10,1... | collective-permute-start | bytes 3145736 | tf_op jit(solution)/shard_map/ppermute | solution.py:19
  129.6 1.4 copy-start.2
  154.4 3.4 %copy-start = (bf16[4096,1024]{1,0:T(8,128)(2,1)}, bf16[4096,1024]{1,0:T(8,128)(2,1)S(1)}, u32[]{:S(2)}) copy-start(bf16[4096,1024]{1,0:T(8,128)(2,1)S(1)} %constant_dynamic-update-slice_fusion) | copy-start | bytes 25165828
